TPU v7x, 256 devices: a whole 4x4x8 slice. The times are simulated.
256 devices in a mesh: dp: 32 (over y, z_hi, x), mp: 8 (over z_lo, core).
Axes of the slice: x: 4, y: 4, z: 8 (z_hi: 2, z_lo: 4; z = z_hi * 4 + z_lo), core: 2. Of those that a mesh axis runs over, the one named last changes fastest.
Arguments:
- tokens: bfloat16 [2048, 6144], P('dp', 'mp'), may hold values from -60 to 60
- norm_gain: float32 [6144], P('mp'), may hold values from 0.5 to 1.5
- w_in: bfloat16 [6144, 24576], P('mp', 'dp'), may hold values from -0.078125 to 0.078125
- b_in: float32 [24576], P('dp'), may hold values from -4 to 4
- w_out: bfloat16 [24576, 6144], P('dp', 'mp'), may hold values from -0.0390625 to 0.0390625
- b_out: float32 [6144], P('mp'), may hold values from -3 to 3
- out_gain: float32 [6144], P('mp'), may hold values from 0.5 to 1.5
- student: bfloat16 [2048, 1024], P(('dp', 'mp')), may hold values from -45 to 45
- w_exit: bfloat16 [1024, 6144], P(None, 'mp'), may hold values from -0.1875 to 0.1875
Outputs:
- mean_loss: float32 [], replicated
- grad_exit: float32 [1024, 6144], P('dp', 'mp')
- grad_student: float32 [2048, 1024], P(('dp', 'mp'))
All inputs are finite; a program needn't handle non-finite values.
Results may differ from a plain program's by a relative error of at most 0.0017.
Values may be sent and summed in bfloat16 or wider, within the bound.
A program may use at most 64 MiB of HBM per device.

v0:
```python
import jax
import jax.numpy as jnp
from jax import lax
from jax.sharding import PartitionSpec as P

epsilon = 1e-06


def shards(tokens, norm_gain, w_in, b_in, w_out, b_out, out_gain, student, w_exit):
    own_rows = tokens.shape[0]
    feature_count = tokens.shape[1] * lax.axis_size("mp")
    total_rows = own_rows * lax.axis_size("dp")
    inputs = tokens.astype(jnp.float32)
    squares = lax.psum(jnp.sum(inputs * inputs, axis=1), "mp")
    scale_in = lax.rsqrt(squares / feature_count + epsilon)
    normed = (inputs * scale_in[:, None] * norm_gain).astype(jnp.bfloat16)
    partial_pre = jnp.dot(
        lax.all_gather(normed, "dp", axis=0, tiled=True), w_in, preferred_element_type=jnp.float32
    )
    preact = lax.psum(partial_pre, "mp") + b_in
    hidden = jax.nn.gelu(preact, approximate=False).astype(jnp.bfloat16)
    rows_now = hidden
    branch = lax.psum_scatter(
        jnp.dot(rows_now, w_out, preferred_element_type=jnp.float32),
        "dp",
        scatter_dimension=0,
        tiled=True,
    )
    features = inputs + branch + b_out
    out_squares = lax.psum(jnp.sum(features * features, axis=1), "mp")
    target = features * lax.rsqrt(out_squares / feature_count + epsilon)[:, None] * out_gain
    learner = lax.all_gather(student, "mp", axis=0, tiled=True)
    predicted = jnp.dot(learner, w_exit, preferred_element_type=jnp.float32)
    errors = predicted - target
    error_sum = lax.psum(jnp.sum(errors * errors), ("dp", "mp"))
    mean_loss = error_sum / (total_rows * feature_count)
    signal = (2.0 * errors).astype(jnp.bfloat16)
    rows_now = signal
    grad_student = lax.psum_scatter(
        lax.dot_general(
            rows_now, w_exit, (((1,), (1,)), ((), ())), preferred_element_type=jnp.float32
        ),
        "mp",
        scatter_dimension=0,
        tiled=True,
    )
    grad_exit = lax.psum_scatter(
        lax.dot_general(
            learner, signal, (((0,), (0,)), ((), ())), preferred_element_type=jnp.float32
        ),
        "dp",
        scatter_dimension=0,
        tiled=True,
    )
    return (mean_loss, grad_exit / total_rows, grad_student)


def solution(mesh):
    placed = (
        P("dp", "mp"),
        P("mp"),
        P("mp", "dp"),
        P("dp"),
        P("dp", "mp"),
        P("mp"),
        P("mp"),
        P(("dp", "mp"), None),
        P(None, "mp"),
    )
    return jax.shard_map(
        shards,
        mesh=mesh,
        in_specs=placed,
        out_specs=(P(), P("dp", "mp"), P(("dp", "mp"), None)),
        check_vma=False,
    )
```

profile of v0, /device:TPU:2, one launch (start us, length us, event | category | flops | bytes accessed | tf_op | source)
XLA Modules:
  0.0 883.0 jit_solution(1066511788309045295)
XLA Ops:
  7.2 0.0 copy-start
  7.2 0.0 all-gather.2.cloned.1.call-start
  7.2 1.1 fusion.12
  8.4 17.6 %psum.28 = f32[64]{0:T(128)S(1)} all-reduce(f32[64]{0:T(128)S(1)} %fusion.12), channel_id=1, replica_groups=mesh['dp'=32,'mp'=8] {'mp'}, use_global_device_ids=true, to_apply=%region_1.0 | all-reduce | flops 64 | bytes 512 | tf_op jit(solution)/shard_map/psum | solution.py:14
  26.0 1.6 fusion.14
  27.6 0.0 all-gather.2.cloned.1.call-update
  27.7 0.0 all-reduce.2.cloned.1.call-start
  27.7 100.5 %all-gather.2.cloned.1.call-done = bf16[2048,768]{1,0:T(8,128)(2,1)} async-done(((bf16[64,768]{1,0:T(8,128)(2,1)}), bf16[2048,768]{1,0:T(8,128)(2,1)}) %all-gather.2.cloned.1.call-update) | async-done | bytes 3145744 | tf_op jit(solution)/shard_map/all_gather | solution.py:18
  128.2 7.5 fusion.49
  135.7 0.0 all-reduce.2.cloned.1.call-update
  135.7 0.0 reduce-scatter.6.cloned.1.call-start
  135.7 143.8 %all-reduce.2.cloned.1.call-done = f32[2048,768]{1,0:T(8,128)} async-done(((f32[2048,768]{1,0:T(8,128)}), f32[2048,768]{1,0:T(8,128)}) %all-reduce.2.cloned.1.call-update) | async-done | bytes 6291472 | tf_op jit(solution)/shard_map/psum | solution.py:20
  279.6 18.8 %fusion.10 = f32[2048,768]{1,0:T(8,128)} fusion(bf16[768,768]{1,0:T(8,128)(2,1)S(1)} %copy-done.5, f32[2048,768]{1,0:T(8,128)} %all-reduce.2.cloned.1.call-done, f32[768]{0:T(1024)S(1)} %copy-done.6), kind=kOutput, calls=%fused_computation.19 | convolution fusion | flops 2519728128 | bytes 13765632 | tf_op jit(solution)/shard_map/dot_general | solution.py:24
  298.4 0.0 reduce-scatter.6.cloned.1.call-update
  298.4 0.0 reduce-scatter.10.cloned.1.call-start
  298.5 0.6 copy-done.3
  299.1 14.0 %all_gather.6 = bf16[64,1024]{1,0:T(8,128)(2,1)S(1)} all-gather(bf16[8,1024]{1,0:T(8,128)(2,1)S(1)} %copy-done.3), channel_id=1, replica_groups=mesh['dp'=32,'mp'=8] {'mp'}, dimensions={0}, use_global_device_ids=true | all-gather | bytes 147456 | tf_op jit(solution)/shard_map/all_gather | solution.py:32
  313.1 253.0 %reduce-scatter.6.cloned.1.call-done = f32[64,768]{1,0:T(8,128)} async-done(((f32[2048,768]{1,0:T(8,128)}), f32[64,768]{1,0:T(8,128)}) %reduce-scatter.6.cloned.1.call-update) | async-done | bytes 196624 | tf_op jit(solution)/shard_map/reduce_scatter | solution.py:23
  566.1 1.1 multiply_reduce_fusion.1
  567.1 13.6 %psum.30 = f32[64]{0:T(128)S(1)} all-reduce(f32[64]{0:T(128)S(1)} %multiply_reduce_fusion.1), channel_id=1, replica_groups=mesh['dp'=32,'mp'=8] {'mp'}, use_global_device_ids=true, to_apply=%region_5.0 | all-reduce | flops 64 | bytes 512 | tf_op jit(solution)/shard_map/psum | solution.py:30
  580.8 1.9 multiply_reduce_fusion
  582.7 2.3 convolution_bitcast_fusion
  585.0 3.5 copy.14
  588.5 0.0 reduce-scatter.10.cloned.1.call-update
  588.6 0.0 reduce-scatter.8.cloned.1.call-start
  588.6 1.3 fusion.16
  589.9 0.0 reduce-scatter.8.cloned.1.call-update
  590.0 73.5 %psum.31 = f32[]{:T(128)} all-reduce(f32[]{:T(128)} %get-tuple-element.9), channel_id=1, replica_groups=mesh['dp'=32,'mp'=8] {'dp','mp'}, use_global_device_ids=true, to_apply=%region_7.0 | all-reduce | flops 1 | bytes 8 | tf_op jit(solution)/shard_map/psum | solution.py:35
  664.1 177.3 %reduce-scatter.10.cloned.1.call-done = f32[32,768]{1,0:T(8,128)} async-done(((f32[1024,768]{1,0:T(8,128)}), f32[32,768]{1,0:T(8,128)}) %reduce-scatter.10.cloned.1.call-update) | async-done | bytes 98320
  841.4 1.1 copy.15
  842.5 0.8 copy.13
  843.3 32.1 %reduce-scatter.8.cloned.1.call-done = f32[8,1024]{1,0:T(8,128)} async-done(((f32[64,1024]{1,0:T(8,128)}), f32[8,1024]{1,0:T(8,128)}) %reduce-scatter.8.cloned.1.call-update) | async-done | bytes 32784 | tf_op jit(solution)/shard_map/reduce_scatter | solution.py:39
  (15 shorter events, 0.1 us)
Async XLA Ops:
  7.2 573.6 %copy-start = (bf16[1024,768]{1,0:T(8,128)(2,1)S(1)}, bf16[1024,768]{1,0:T(8,128)(2,1)}, u32[]{:S(2)}) copy-start(bf16[1024,768]{1,0:T(8,128)(2,1)} %param.17) | copy-start | bytes 4718596
  7.2 121.0 %all-gather.2.cloned.1.call-start = ((), (), s32[]{:S(2)}) async-start(), calls=%async_computation.3 | async-start | bytes 3244032 | tf_op jit(solution)/shard_map/all_gather | solution.py:18
  27.7 251.9 %all-reduce.2.cloned.1.call-start = ((), (), s32[]{:S(2)}) async-start(), calls=%async_computation.4 | async-start | bytes 12582912 | tf_op jit(solution)/shard_map/psum | solution.py:20
  135.7 143.9 %copy-start.5 = (bf16[768,768]{1,0:T(8,128)(2,1)S(1)}, bf16[768,768]{1,0:T(8,128)(2,1)}, u32[]{:S(2)}) copy-start(bf16[768,768]{1,0:T(8,128)(2,1)} %param.13) | copy-start | bytes 3538948
  135.7 143.9 %copy-start.6 = (f32[768]{0:T(1024)S(1)}, f32[768]{0:T(1024)}, u32[]{:S(2)}) copy-start(f32[768]{0:T(1024)} %param.12) | copy-start | bytes 9220
  135.7 430.4 %reduce-scatter.6.cloned.1.call-start = ((), (), s32[]{:S(2)}) async-start(), calls=%async_computation.5 | async-start | bytes 6488064 | tf_op jit(solution)/shard_map/reduce_scatter | solution.py:23
  298.4 0.7 copy-start.3
  298.4 267.7 %copy-start.1 = (bf16[64,768]{1,0:T(8,128)(2,1)S(1)}, bf16[64,768]{1,0:T(8,128)(2,1)}, u32[]{:S(2)}) copy-start(bf16[64,768]{1,0:T(8,128)(2,1)} %param.9) | copy-start | bytes 294916
  298.4 267.7 %copy-start.2 = (f32[768]{0:T(1024)S(1)}, f32[768]{0:T(1024)}, u32[]{:S(2)}) copy-start(f32[768]{0:T(1024)} %param.14) | copy-start | bytes 9220
  298.4 282.4 %copy-start.4 = (f32[768]{0:T(1024)S(1)}, f32[768]{0:T(1024)}, u32[]{:S(2)}) copy-start(f32[768]{0:T(1024)} %param.15) | copy-start | bytes 9220
  298.4 543.0 %reduce-scatter.10.cloned.1.call-start = ((), (), s32[]{:S(2)}) async-start(), calls=%async_computation.7 | async-start | bytes 3244032
  588.6 286.8 %reduce-scatter.8.cloned.1.call-start = ((), (), s32[]{:S(2)}) async-start(), calls=%async_computation.6 | async-start | bytes 294912 | tf_op jit(solution)/shard_map/reduce_scatter | solution.py:39
Sparse Core Ops, SparseCore 0:
  27.8 100.3 all-gather.1
  135.8 143.7 all-reduce.1
  298.5 267.5 reduce-scatter.5
  588.7 252.6 reduce-scatter.9
  844.4 30.8 reduce-scatter.7
where the time goes:
time: 883 us
  waiting for transfers between devices  707 us (80%)
  blocking collectives  119 us (13%)
  matrix products  31.9 us (4%)
  between operations  15.6 us (2%)
    reduce_scatter x1, waiting for transfers between devices, shards(): lax.psum_scatter(jnp.dot(rows_now, w_out, preferred_element_type=jnp.floa...  253 us
    unnamed x6, waiting for transfers between devices  177 us
    psum x1, waiting for transfers between devices, shards(): preact = lax.psum(partial_pre, 'mp') + b_in  144 us
    all_gather x1, waiting for transfers between devices, shards(): lax.all_gather(normed, 'dp', axis=0, tiled=True)  100 us
    psum x1, blocking collectives, shards(): error_sum = lax.psum(jnp.sum(errors * errors), ('dp', 'mp'))  73.5 us
    reduce_scatter x1, waiting for transfers between devices, shards(): lax.psum_scatter(lax.dot_general(rows_now, w_exit, (((1,), (1,)), ((), ()...  32.1 us
    dot_general x1, matrix products, shards(): jnp.dot(rows_now, w_out, preferred_element_type=jnp.float32)  18.8 us
  transfers between devices with their start and end apart: 5, of which 5 were waited for; matrix products, arithmetic and copies ran while one was open for 0% of the time, Pallas kernels for 0%

commit v1 on v0

--- a/solution.py
+++ b/solution.py
@@ -15,7 +15,11 @@
     scale_in = lax.rsqrt(squares / feature_count + epsilon)
     normed = (inputs * scale_in[:, None] * norm_gain).astype(jnp.bfloat16)
     partial_pre = jnp.dot(
-        lax.all_gather(normed, "dp", axis=0, tiled=True), w_in, preferred_element_type=jnp.float32
+        jnp.concatenate(
+            lax.all_to_all(jnp.stack([normed] * lax.axis_size("dp")), "dp", 0, 0), axis=0
+        ),
+        w_in,
+        preferred_element_type=jnp.float32,
     )
     preact = lax.psum(partial_pre, "mp") + b_in
     hidden = jax.nn.gelu(preact, approximate=False).astype(jnp.bfloat16)

time: 883 us -> 864 us (0.978)
  waiting for transfers between devices: 707 us -> 609 us
  blocking collectives: 119 us -> 201 us
    all_gather x1 -> x0, waiting for transfers between devices: 100 us -> none  [shards(): lax.all_gather(normed, 'dp', axis=0, tiled=True)]
    all_to_all x0 -> x1, blocking collectives: none -> 82.2 us  [shards(): lax.all_to_all(jnp.stack([normed] * lax.axis_size('dp')), 'dp', 0, 0)]
    unnamed x6 -> x5, waiting for transfers between devices: 177 us -> 177 us
  transfers between devices with their start and end apart: 5 -> 4, of which waited for: 5 -> 4; matrix products, arithmetic and copies ran while one was open for 0% -> 0% of each run, Pallas kernels for 0% -> 0%
where the time goes in v1:
time: 864 us
  waiting for transfers between devices  609 us (70%)
  blocking collectives  201 us (23%)
  matrix products  28.8 us (3%)
  between operations  15.6 us (2%)
    reduce_scatter x1, waiting for transfers between devices, shards(): lax.psum_scatter(jnp.dot(rows_now, w_out, preferred_element_type=jnp.floa...  253 us
    unnamed x5, waiting for transfers between devices  177 us
    psum x1, waiting for transfers between devices, shards(): preact = lax.psum(partial_pre, 'mp') + b_in  146 us
    all_to_all x1, blocking collectives, shards(): lax.all_to_all(jnp.stack([normed] * lax.axis_size('dp')), 'dp', 0, 0)  82.2 us
    psum x1, blocking collectives, shards(): error_sum = lax.psum(jnp.sum(errors * errors), ('dp', 'mp'))  73.5 us
    reduce_scatter x1, waiting for transfers between devices, shards(): lax.psum_scatter(lax.dot_general(rows_now, w_exit, (((1,), (1,)), ((), ()...  32.1 us
    dot_general x1, matrix products, shards(): jnp.dot(rows_now, w_out, preferred_element_type=jnp.float32)  18.8 us
    psum x1, blocking collectives, shards(): squares = lax.psum(jnp.sum(inputs * inputs, axis=1), 'mp')  17.6 us
  transfers between devices with their start and end apart: 4, of which 4 were waited for; matrix products, arithmetic and copies ran while one was open for 0% of the time, Pallas kernels for 0%

profile of v1, /device:TPU:2, one launch (start us, length us, event | category | flops | bytes accessed | tf_op | source)
XLA Modules:
  0.0 863.9 jit_solution(13470432744026913785)
XLA Ops:
  7.2 0.0 copy-start
  7.2 0.0 copy-start.5
  7.2 0.0 all-reduce.2.cloned.1.call-start
  7.2 1.2 fusion.12
  8.4 17.6 %psum.28 = f32[64]{0:T(128)S(1)} all-reduce(f32[64]{0:T(128)S(1)} %fusion.12), channel_id=1, replica_groups=mesh['dp'=32,'mp'=8] {'mp'}, use_global_device_ids=true, to_apply=%region_1.0 | all-reduce | flops 64 | bytes 512 | tf_op jit(solution)/shard_map/psum | solution.py:14
  26.1 1.0 fusion.14
  27.1 0.3 stack.2
  27.4 82.2 %all_to_all.5 = bf16[32,64,768]{2,1,0:T(8,128)(2,1)S(1)} all-to-all(bf16[32,64,768]{2,1,0:T(8,128)(2,1)S(1)} %stack.2), channel_id=1, replica_groups=mesh['dp'=32,'mp'=8] {'dp'}, dimensions={0} | all-to-all | bytes 6291456 | tf_op jit(solution)/shard_map/all_to_all | solution.py:19
  109.6 4.4 fusion.49
  114.1 0.0 all-reduce.2.cloned.1.call-update
  114.1 0.0 reduce-scatter.6.cloned.1.call-start
  114.1 146.4 %all-reduce.2.cloned.1.call-done = f32[2048,768]{1,0:T(8,128)} async-done(((f32[2048,768]{1,0:T(8,128)}), f32[2048,768]{1,0:T(8,128)}) %all-reduce.2.cloned.1.call-update) | async-done | bytes 6291472 | tf_op jit(solution)/shard_map/psum | solution.py:24
  260.5 18.8 %fusion.10 = f32[2048,768]{1,0:T(8,128)} fusion(bf16[768,768]{1,0:T(8,128)(2,1)S(1)} %copy-done.6, f32[2048,768]{1,0:T(8,128)} %all-reduce.2.cloned.1.call-done, f32[768]{0:T(1024)S(1)} %copy-done.7), kind=kOutput, calls=%fused_computation.19 | convolution fusion | flops 2519728128 | bytes 13765632 | tf_op jit(solution)/shard_map/dot_general | solution.py:28
  279.3 0.0 reduce-scatter.6.cloned.1.call-update
  279.4 0.0 reduce-scatter.10.cloned.1.call-start
  279.4 0.6 copy-done.3
  280.0 14.0 %all_gather.3 = bf16[64,1024]{1,0:T(8,128)(2,1)S(1)} all-gather(bf16[8,1024]{1,0:T(8,128)(2,1)S(1)} %copy-done.3), channel_id=1, replica_groups=mesh['dp'=32,'mp'=8] {'mp'}, dimensions={0}, use_global_device_ids=true | all-gather | bytes 147456 | tf_op jit(solution)/shard_map/all_gather | solution.py:36
  294.0 252.9 %reduce-scatter.6.cloned.1.call-done = f32[64,768]{1,0:T(8,128)} async-done(((f32[2048,768]{1,0:T(8,128)}), f32[64,768]{1,0:T(8,128)}) %reduce-scatter.6.cloned.1.call-update) | async-done | bytes 196624 | tf_op jit(solution)/shard_map/reduce_scatter | solution.py:27
  546.9 1.1 multiply_reduce_fusion.1
  548.0 13.6 %psum.30 = f32[64]{0:T(128)S(1)} all-reduce(f32[64]{0:T(128)S(1)} %multiply_reduce_fusion.1), channel_id=1, replica_groups=mesh['dp'=32,'mp'=8] {'mp'}, use_global_device_ids=true, to_apply=%region_5.0 | all-reduce | flops 64 | bytes 512 | tf_op jit(solution)/shard_map/psum | solution.py:34
  561.6 1.9 multiply_reduce_fusion
  563.5 2.3 convolution_bitcast_fusion
  565.8 3.5 copy.14
  569.4 0.0 reduce-scatter.10.cloned.1.call-update
  569.4 0.0 reduce-scatter.8.cloned.1.call-start
  569.4 1.3 fusion.16
  570.8 0.0 reduce-scatter.8.cloned.1.call-update
  570.8 73.5 %psum.31 = f32[]{:T(128)} all-reduce(f32[]{:T(128)} %get-tuple-element.9), channel_id=1, replica_groups=mesh['dp'=32,'mp'=8] {'dp','mp'}, use_global_device_ids=true, to_apply=%region_7.0 | all-reduce | flops 1 | bytes 8 | tf_op jit(solution)/shard_map/psum | solution.py:39
  644.9 177.4 %reduce-scatter.10.cloned.1.call-done = f32[32,768]{1,0:T(8,128)} async-done(((f32[1024,768]{1,0:T(8,128)}), f32[32,768]{1,0:T(8,128)}) %reduce-scatter.10.cloned.1.call-update) | async-done | bytes 98320
  822.3 1.1 copy.15
  823.4 0.8 copy.13
  824.2 32.1 %reduce-scatter.8.cloned.1.call-done = f32[8,1024]{1,0:T(8,128)} async-done(((f32[64,1024]{1,0:T(8,128)}), f32[8,1024]{1,0:T(8,128)}) %reduce-scatter.8.cloned.1.call-update) | async-done | bytes 32784 | tf_op jit(solution)/shard_map/reduce_scatter | solution.py:43
  (16 shorter events, 0.1 us)
Async XLA Ops:
  7.2 554.4 %copy-start = (bf16[1024,768]{1,0:T(8,128)(2,1)S(1)}, bf16[1024,768]{1,0:T(8,128)(2,1)}, u32[]{:S(2)}) copy-start(bf16[1024,768]{1,0:T(8,128)(2,1)} %param.17) | copy-start | bytes 4718596
  7.2 102.4 %copy-start.5 = (bf16[768,768]{1,0:T(8,128)(2,1)S(1)}, bf16[768,768]{1,0:T(8,128)(2,1)}, u32[]{:S(2)}) copy-start(bf16[768,768]{1,0:T(8,128)(2,1)} %param.11) | copy-start | bytes 3538948
  7.2 253.3 %all-reduce.2.cloned.1.call-start = ((), (), s32[]{:S(2)}) async-start(), calls=%async_computation.4 | async-start | bytes 12582912 | tf_op jit(solution)/shard_map/psum | solution.py:24
  114.1 146.5 %copy-start.6 = (bf16[768,768]{1,0:T(8,128)(2,1)S(1)}, bf16[768,768]{1,0:T(8,128)(2,1)}, u32[]{:S(2)}) copy-start(bf16[768,768]{1,0:T(8,128)(2,1)} %param.13) | copy-start | bytes 3538948
  114.1 146.5 %copy-start.7 = (f32[768]{0:T(1024)S(1)}, f32[768]{0:T(1024)}, u32[]{:S(2)}) copy-start(f32[768]{0:T(1024)} %param.12) | copy-start | bytes 9220
  114.1 432.8 %reduce-scatter.6.cloned.1.call-start = ((), (), s32[]{:S(2)}) async-start(), calls=%async_computation.5 | async-start | bytes 6488064 | tf_op jit(solution)/shard_map/reduce_scatter | solution.py:27
  279.3 0.7 copy-start.3
  279.3 267.6 %copy-start.1 = (bf16[64,768]{1,0:T(8,128)(2,1)S(1)}, bf16[64,768]{1,0:T(8,128)(2,1)}, u32[]{:S(2)}) copy-start(bf16[64,768]{1,0:T(8,128)(2,1)} %param.9) | copy-start | bytes 294916
  279.3 267.6 %copy-start.2 = (f32[768]{0:T(1024)S(1)}, f32[768]{0:T(1024)}, u32[]{:S(2)}) copy-start(f32[768]{0:T(1024)} %param.14) | copy-start | bytes 9220
  279.3 282.2 %copy-start.4 = (f32[768]{0:T(1024)S(1)}, f32[768]{0:T(1024)}, u32[]{:S(2)}) copy-start(f32[768]{0:T(1024)} %param.15) | copy-start | bytes 9220
  279.4 542.9 %reduce-scatter.10.cloned.1.call-start = ((), (), s32[]{:S(2)}) async-start(), calls=%async_computation.7 | async-start | bytes 3244032
  569.4 286.8 %reduce-scatter.8.cloned.1.call-start = ((), (), s32[]{:S(2)}) async-start(), calls=%async_computation.6 | async-start | bytes 294912 | tf_op jit(solution)/shard_map/reduce_scatter | solution.py:43
Sparse Core Ops, SparseCore 0:
  114.2 146.2 all-reduce.1
  279.5 267.3 reduce-scatter.5
  569.5 252.7 reduce-scatter.9
  825.4 30.8 reduce-scatter.7
